TPU v7x, 256 devices: a whole 4x4x8 slice. The times are simulated.
256 devices in a mesh: dp: 32 (over x, z_lo, core), ctx: 8 (over z_hi, y).
Axes of the slice: x: 4, y: 4, z: 8 (z_hi: 2, z_lo: 4; z = z_hi * 4 + z_lo), core: 2. Of those that a mesh axis runs over, the one named last changes fastest.
Arguments:
- queries: bfloat16 [32768, 4096], P(('dp', 'ctx')), may hold values from -10 to 10
- keys: bfloat16 [32768, 4096], P(('dp', 'ctx')), may hold values from -10 to 10
- values: bfloat16 [32768, 4096], P(('dp', 'ctx')), may hold values from -6 to 6
- residual_in: bfloat16 [32768, 7168], P(('dp', 'ctx')), may hold values from -40 to 40
- out_weight: bfloat16 [4096, 7168], P('ctx', 'dp'), may hold values from -1.25 to 1.25
- norm_gain: float32 [7168], replicated, may hold values from 0.5 to 1.5
- norm_bias: float32 [7168], replicated, may hold values from -3 to 3
Outputs:
- layer_out: bfloat16 [32768, 7168], P(('dp', 'ctx'))
All inputs are finite; a program needn't handle non-finite values.
Results may differ from a plain program's by a relative error of at most 0.0085.
Values may be sent and summed in bfloat16 or wider, within the bound.
No kernel may reach another device: no remote copies, remote signals or barrier semaphores. Data moves between devices by JAX's collectives and lax.ppermute only.
A program may use at most 128 MiB of HBM per device.

v0:
```python
import math

import jax
import jax.numpy as jnp
from jax import lax
from jax.sharding import PartitionSpec as P

HEADS = 32


deepnorm_alpha = 96.0**0.25
norm_eps = 1e-05


def block_rows(length):
    block = min(512, length)
    while length % block != 0:
        block = block + 1
    return block


def attend(all_queries, all_keys, all_values, local_heads):
    length = all_queries.shape[0]
    width = all_queries.shape[1]
    head_dim = width // local_heads
    block = block_rows(length)
    blocks = length // block
    scale = 1.0 / math.sqrt(head_dim)
    query_blocks = all_queries.reshape(blocks, block, local_heads, head_dim)
    key_heads = all_keys.reshape(length, local_heads, head_dim)
    value_heads = all_values.reshape(length, local_heads, head_dim)
    key_position = jnp.arange(length)

    def one_block(inputs):
        number, query_part = inputs
        scores = (
            jnp.einsum("qhd,khd->hqk", query_part, key_heads, preferred_element_type=jnp.float32)
            * scale
        )
        query_position = number * block + jnp.arange(block)
        causal = query_position[:, None] >= key_position[None, :]
        scores = jnp.where(causal[None], scores, -1e30)
        highest = jnp.max(scores, axis=-1, keepdims=True)
        expo = jnp.exp(scores - highest)
        probs = (expo / jnp.sum(expo, axis=-1, keepdims=True)).astype(jnp.bfloat16)
        result = jnp.einsum("hqk,khd->qhd", probs, value_heads, preferred_element_type=jnp.float32)
        return result.astype(jnp.bfloat16).reshape(block, width)

    outputs = lax.map(one_block, (jnp.arange(blocks), query_blocks))
    return outputs.reshape(length, width)


def local(queries, keys, values, residual_in, out_weight, norm_gain, norm_bias):
    head_q, head_k, head_v = (
        lax.all_to_all(queries, "ctx", split_axis=1, concat_axis=0, tiled=True),
        lax.all_to_all(keys, "ctx", split_axis=1, concat_axis=0, tiled=True),
        lax.all_to_all(values, "ctx", split_axis=1, concat_axis=0, tiled=True),
    )
    groups = lax.axis_size("ctx")
    attn_heads = attend(head_q, head_k, head_v, HEADS // groups)
    group_rows = lax.all_gather(out_weight, "dp", axis=1, tiled=True)
    summed = lax.psum_scatter(
        jnp.dot(attn_heads, group_rows, preferred_element_type=jnp.float32).astype(jnp.bfloat16),
        "ctx",
        scatter_dimension=0,
        tiled=True,
    )
    attn_float = lax.optimization_barrier(summed).astype(jnp.float32)
    mixed = deepnorm_alpha * residual_in.astype(jnp.float32) + attn_float
    mean = jnp.mean(mixed, axis=-1, keepdims=True)
    centered = mixed - mean
    var = jnp.mean(centered * centered, axis=-1, keepdims=True)
    normed = centered * lax.rsqrt(var + norm_eps) * norm_gain + norm_bias
    return normed.astype(jnp.bfloat16)


def solution(mesh):
    in_specs = (
        P(("dp", "ctx"), None),
        P(("dp", "ctx"), None),
        P(("dp", "ctx"), None),
        P(("dp", "ctx"), None),
        P("ctx", "dp"),
        P(),
        P(),
    )
    out_specs = P(("dp", "ctx"), None)
    return jax.shard_map(local, mesh=mesh, in_specs=in_specs, out_specs=out_specs, check_vma=False)
```

profile of v0, /device:TPU:1, one launch (start us, length us, event | category | flops | bytes accessed | tf_op | source)
XLA Modules:
  0.0 447.7 jit_solution(4271503667197037777)
XLA Ops:
  6.5 0.7 all-gather.2.cloned.1.call-update
  7.3 2.3 copy.46
  9.6 11.6 %all-to-all-start = ((bf16[128,8,512]{2,0,1:T(8,128)(2,1)}), bf16[128,8,512]{2,0,1:T(8,128)(2,1)S(1)}, u32[]{:S(2)}, u32[]{:S(2)}) async-start(bf16[128,8,512]{2,0,1:T(8,128)(2,1)} %bitcast.34), calls=%async_computation | async-start | bytes 2097152 | tf_op jit(solution)/shard_map/all_to_all | solution.py:55
  21.2 1.3 copy.23
  22.5 28.0 %all-to-all-done = bf16[128,8,512]{2,0,1:T(8,128)(2,1)S(1)} async-done(((bf16[128,8,512]{2,0,1:T(8,128)(2,1)}), bf16[128,8,512]{2,0,1:T(8,128)(2,1)S(1)}, u32[]{:S(2)}, u32[]{:S(2)}) %all-to-all-start) | async-done | bytes 1048608 | tf_op jit(solution)/shard_map/all_to_all | solution.py:55
  50.5 4.4 all-to-all-start.1
  55.0 2.3 copy.25
  57.2 23.6 %all-to-all-done.1 = bf16[128,8,512]{0,2,1:T(8,128)(2,1)S(1)} async-done(((bf16[128,8,512]{0,2,1:T(8,128)(2,1)}), bf16[128,8,512]{0,2,1:T(8,128)(2,1)S(1)}, u32[]{:S(2)}, u32[]{:S(2)}) %all-to-all-start.1) | async-done | bytes 1048608 | tf_op jit(solution)/shard_map/all_to_all | solution.py:56
  80.9 6.8 %all-to-all-start.2 = ((bf16[128,8,512]{0,2,1:T(8,128)(2,1)}), bf16[128,8,512]{0,2,1:T(8,128)(2,1)}, u32[]{:S(2)}, u32[]{:S(2)}) async-start(bf16[128,8,512]{0,2,1:T(8,128)(2,1)} %bitcast.3), calls=%async_computation.2 | async-start | bytes 2097152 | tf_op jit(solution)/shard_map/all_to_all | solution.py:57
  88.0 0.7 copy.24
  88.7 0.5 reshape.77
  89.2 1.3 copy.28
  90.5 16.4 %all-to-all-done.2 = bf16[128,8,512]{0,2,1:T(8,128)(2,1)} async-done(((bf16[128,8,512]{0,2,1:T(8,128)(2,1)}), bf16[128,8,512]{0,2,1:T(8,128)(2,1)}, u32[]{:S(2)}, u32[]{:S(2)}) %all-to-all-start.2) | async-done | bytes 1048608 | tf_op jit(solution)/shard_map/all_to_all | solution.py:57
  106.9 1.9 copy.26
  108.8 1.3 reshape.78
  110.1 27.0 %while.11 = (s32[]{:T(128)}, bf16[2,512,512]{2,1,0:T(8,128)(2,1)}, s32[2]{0:T(128)S(1)}, bf16[2,512,4,128]{3,2,1,0:T(4,128)(2,1)S(1)}, bf16[1024,4,128]{2,0,1:T(...) while((s32[]{:T(128)}, bf16[2,512,512]{2,1,0:T(8,128)(2,1)}, ...), condition=%wide.region_3.4_spmd.clone, body=%wide.region_0.3_spmd.clone.sunk | while | flops 1087112704 | bytes 24137856 | solution.py:49
  110.1 0.6 dynamic_slice.14
  111.3 0.4 iota_compare_fusion.2
  111.9 5.4 %fusion.27 = (f32[4,512]{1,0:T(4,128)S(1)}, f32[4,512,1024]{2,1,0:T(8,128)}) fusion(pred[512,1024]{1,0:T(8,128)(4,1)S(1)} %iota_compare_fusion.2, bf16[1024,4,128]{2,0,1:T(8,128)(2,1)S(1)} %get-tuple-element.150, bf16[1,512,4,128]{3,2,1,0:T(4,128)(2,1)S(1)} %constant_dynamic-slice_fusion.2), kind=kOutput, calls=%fused_computation.28.clone.1 | convolution fusion | flops 545260544 | bytes 10493952 | tf_op jit(solution)/shard_map/while/body/eval_jaxpr/sub | solution.py:44
  117.3 5.3 %fusion.28 = bf16[4,512,128]{1,2,0:T(8,128)(2,1)S(1)} fusion(bf16[1024,4,128]{0,2,1:T(8,128)(2,1)} %get-tuple-element.151, f32[4,512,1024]{2,1,0:T(8,128)} %get-tuple-element.128, f32[4,512]{1,0:T(4,128)S(1)} %get-tuple-element.129), kind=kOutput, calls=%fused_computation.11.clone.1 | convolution fusion | flops 541327360 | bytes 9969664 | tf_op jit(solution)/shard_map/while/body/eval_jaxpr/hqk,khd->qhd/dot_general | solution.py:46
  122.8 0.8 constant_dynamic-update-slice_fusion.2
  123.6 0.6 dynamic_slice.14
  124.8 0.4 iota_compare_fusion.2
  125.3 5.4 %fusion.27 = (f32[4,512]{1,0:T(4,128)S(1)}, f32[4,512,1024]{2,1,0:T(8,128)}) fusion(pred[512,1024]{1,0:T(8,128)(4,1)S(1)} %iota_compare_fusion.2, bf16[1024,4,128]{2,0,1:T(8,128)(2,1)S(1)} %get-tuple-element.150, bf16[1,512,4,128]{3,2,1,0:T(4,128)(2,1)S(1)} %constant_dynamic-slice_fusion.2), kind=kOutput, calls=%fused_computation.28.clone.1 | convolution fusion | flops 545260544 | bytes 10493952 | tf_op jit(solution)/shard_map/while/body/eval_jaxpr/sub | solution.py:44
  130.8 5.4 %fusion.28 = bf16[4,512,128]{1,2,0:T(8,128)(2,1)S(1)} fusion(bf16[1024,4,128]{0,2,1:T(8,128)(2,1)} %get-tuple-element.151, f32[4,512,1024]{2,1,0:T(8,128)} %get-tuple-element.128, f32[4,512]{1,0:T(4,128)S(1)} %get-tuple-element.129), kind=kOutput, calls=%fused_computation.11.clone.1 | convolution fusion | flops 541327360 | bytes 9969664 | tf_op jit(solution)/shard_map/while/body/eval_jaxpr/hqk,khd->qhd/dot_general | solution.py:46
  136.3 0.8 constant_dynamic-update-slice_fusion.2
  137.2 7.5 %all-gather.2.cloned.1.call-done = bf16[512,7168]{0,1:T(8,128)(2,1)} async-done(((bf16[512,224]{0,1:T(8,128)(2,1)}), bf16[512,7168]{0,1:T(8,128)(2,1)}) %all-gather.2.cloned.1.call-update) | async-done | bytes 7340048 | tf_op jit(solution)/shard_map/all_gather | solution.py:61
  144.7 13.3 %convolution_convert_fusion = bf16[1024,7168]{1,0:T(8,128)(2,1)} fusion(bf16[1024,512]{1,0:T(8,128)(2,1)} %bitcast.49, bf16[512,7168]{0,1:T(8,128)(2,1)} %all-gather.2.cloned.1.call-done), kind=kOutput, calls=%fused_computation.20 | convolution fusion | flops 7523532800 | bytes 23068672 | tf_op jit(solution)/shard_map/dot_general | solution.py:63
  158.1 277.3 %reduce-scatter.2.cloned.1.call-done = bf16[128,7168]{1,0:T(8,128)(2,1)} async-done(((bf16[1024,7168]{1,0:T(8,128)(2,1)}), bf16[128,7168]{1,0:T(8,128)(2,1)}) %reduce-scatter.2.cloned.1.call-update) | async-done | bytes 1835024 | tf_op jit(solution)/shard_map/reduce_scatter | solution.py:62
  435.3 2.3 fusion.14
  437.7 0.9 multiply_reduce_fusion
  438.6 2.3 add_convert_fusion
  (26 shorter events, 1.2 us)
Async XLA Ops:
  6.5 14.7 %copy-start.2 = (bf16[128,4096]{1,0:T(8,128)(2,1)S(1)}, bf16[128,4096]{1,0:T(8,128)(2,1)}, u32[]{:S(2)}) copy-start(bf16[128,4096]{1,0:T(8,128)(2,1)} %param.10) | copy-start | bytes 3145732
  6.5 138.1 %all-gather.2.cloned.1.call-start = ((), (), s32[]{:S(2)}) async-start(), calls=%async_computation.4 | async-start | bytes 7569408 | tf_op jit(solution)/shard_map/all_gather | solution.py:61
  9.6 41.0 %all-to-all-start = ((bf16[128,8,512]{2,0,1:T(8,128)(2,1)}), bf16[128,8,512]{2,0,1:T(8,128)(2,1)S(1)}, u32[]{:S(2)}, u32[]{:S(2)}) async-start(bf16[128,8,512]{2,0,1:T(8,128)(2,1)} %bitcast.34), calls=%async_computation | async-start | bytes 2097152 | tf_op jit(solution)/shard_map/all_to_all | solution.py:55
  50.5 30.3 %all-to-all-start.1 = ((bf16[128,8,512]{0,2,1:T(8,128)(2,1)}), bf16[128,8,512]{0,2,1:T(8,128)(2,1)S(1)}, u32[]{:S(2)}, u32[]{:S(2)}) async-start(bf16[128,8,512]{0,2,1:T(8,128)(2,1)} %bitcast.1), calls=%async_computation.1 | async-start | bytes 2097152 | tf_op jit(solution)/shard_map/all_to_all | solution.py:56
  80.9 26.1 %all-to-all-start.2 = ((bf16[128,8,512]{0,2,1:T(8,128)(2,1)}), bf16[128,8,512]{0,2,1:T(8,128)(2,1)}, u32[]{:S(2)}, u32[]{:S(2)}) async-start(bf16[128,8,512]{0,2,1:T(8,128)(2,1)} %bitcast.3), calls=%async_computation.2 | async-start | bytes 2097152 | tf_op jit(solution)/shard_map/all_to_all | solution.py:57
  87.6 347.7 %reduce-scatter.2.cloned.1.call-start = ((), (), s32[]{:S(2)}) async-start(), calls=%async_computation.5 | async-start | bytes 16515072 | tf_op jit(solution)/shard_map/reduce_scatter | solution.py:62
  90.5 19.7 %copy-start.3 = (bf16[1024,4,128]{2,0,1:T(8,128)(2,1)S(1)}, bf16[1024,4,128]{2,0,1:T(8,128)(2,1)}, u32[]{:S(2)}) copy-start(bf16[1024,4,128]{2,0,1:T(8,128)(2,1)} %copy.28) | copy-start | bytes 3145732
  158.0 277.3 %copy-start = (bf16[128,7168]{1,0:T(8,128)(2,1)S(1)}, bf16[128,7168]{1,0:T(8,128)(2,1)}, u32[]{:S(2)}) copy-start(bf16[128,7168]{1,0:T(8,128)(2,1)} %param.12) | copy-start | bytes 5505028
  158.0 280.6 %copy-start.4 = (f32[7168]{0:T(1024)S(1)}, f32[7168]{0:T(1024)}, u32[]{:S(2)}) copy-start(f32[7168]{0:T(1024)} %param.15) | copy-start | bytes 86020
  158.1 280.6 %copy-start.5 = (f32[7168]{0:T(1024)S(1)}, f32[7168]{0:T(1024)}, u32[]{:S(2)}) copy-start(f32[7168]{0:T(1024)} %param.14) | copy-start | bytes 86020
  435.3 2.3 copy-start.1
Sparse Core Ops, SparseCore 0:
  9.2 135.4 all-gather.1
  158.2 277.1 reduce-scatter.1
where the time goes:
time: 448 us
  waiting for transfers between devices  354 us (79%)
  matrix products  34.8 us (8%)
  starting transfers between devices  22.9 us (5%)
  local copies, waits for them, and re-layouts  15.5 us (3%)
  between operations  13.5 us (3%)
  other arithmetic  6.24 us (1%)
    reduce_scatter x1, waiting for transfers between devices, local(): lax.psum_scatter(jnp.dot(attn_heads, group_rows, preferred_element_type=j...  277 us
    all_to_all x1, waiting for transfers between devices, local(): lax.all_to_all(queries, 'ctx', split_axis=1, concat_axis=0, tiled=True)  28 us
    all_to_all x1, waiting for transfers between devices, local(): lax.all_to_all(keys, 'ctx', split_axis=1, concat_axis=0, tiled=True)  23.6 us
    all_to_all x1, waiting for transfers between devices, local(): lax.all_to_all(values, 'ctx', split_axis=1, concat_axis=0, tiled=True)  16.4 us
    dot_general x1, matrix products, local(): jnp.dot(attn_heads, group_rows, preferred_element_type=jnp.float32)  13.3 us
    all_to_all x1, starting transfers between devices, local(): lax.all_to_all(queries, 'ctx', split_axis=1, concat_axis=0, tiled=True)  11.6 us
    sub x2, matrix products, one_block(): expo = jnp.exp(scores - highest)  10.8 us
    dot_general x2, matrix products, one_block(): jnp.einsum('hqk,khd->qhd', probs, value_heads, preferred_element_type=jnp...  10.7 us
  transfers between devices with their start and end apart: 5, of which 5 were waited for; matrix products, arithmetic and copies ran while one was open for 8% of the time, Pallas kernels for 0%

commit v1 on v0

v1 whole, which is shorter than its diff:
```python
import functools
import math

import jax
import jax.numpy as jnp
from jax import lax
from jax.experimental import pallas as pl
from jax.experimental.pallas import tpu as pltpu
from jax.sharding import Mesh, PartitionSpec as P

HD = 128
GROUP = 512
ROWS = 128
SEQ_HALF = 512
D = 7168
HALF = D // 2

deepnorm_alpha = 96.0**0.25
norm_eps = 1e-05
score_scale = math.log2(math.e) / math.sqrt(HD)

AXES = ("x", "zl", "c", "zh", "y")


def ring(n, step):
    return [(i, (i + step) % n) for i in range(n)]


def spread_pairs(flip):
    pairs = []
    for s in range(32):
        half = (s // 8 % 2) ^ flip
        place = s % 8 * 2 + half
        pairs.append((s, (place % 4) * 8 + (place // 4) * 2 + s // 16))
    return pairs


def softmax_part(q, k, v, keep):
    scores = lax.dot_general(k, q, (((1,), (1,)), ((), ())), preferred_element_type=jnp.float32)
    if keep is not None:
        scores = jnp.where(keep, scores, -1e30)
    highest = jnp.max(scores, axis=0, keepdims=True)
    expo = jnp.exp2((scores - highest) * score_scale)
    total = jnp.sum(expo, axis=0, keepdims=True)
    out = lax.dot_general(
        v, expo.astype(jnp.bfloat16), (((0,), (0,)), ((), ())), preferred_element_type=jnp.float32
    )
    return (out / total).astype(jnp.bfloat16), highest * score_scale + jnp.log2(total)


def own_kernel(where_ref, *refs):
    q_refs, k_refs, v_refs, o_ref, lse_ref = refs[0:4], refs[4:8], refs[8:12], refs[12], refs[13]
    head = pl.program_id(0)
    y = where_ref[0]
    q, k, v = (jnp.concatenate([r[...] for r in part], axis=0) for part in (q_refs, k_refs, v_refs))

    def position(axis):
        at = lax.broadcasted_iota(jnp.int32, (SEQ_HALF, SEQ_HALF), axis)
        return ((y - at // ROWS) & 3) * ROWS + (at & (ROWS - 1))

    out, lse = softmax_part(q, k, v, position(0) <= position(1))
    o_ref[...] = out
    lse_ref[pl.ds(head, 1), :] = lse


def far_kernel(where_ref, q_ref, *refs):
    k_refs, v_refs, o_ref, lse_ref = refs[0:4], refs[4:8], refs[8], refs[9]
    head = pl.program_id(0)

    @pl.when(where_ref[1] == 0)
    def _():
        k, v = (jnp.concatenate([r[...] for r in part], axis=0) for part in (k_refs, v_refs))
        out, lse = softmax_part(q_ref[...], k, v, None)
        o_ref[pl.ds(pl.multiple_of(head * HD, HD), HD), :] = out
        lse_ref[pl.ds(head, 1), :] = lse

        @pl.when(head == GROUP // HD - 1)
        def _():
            rest = lse_ref[0:4, :]
            terms = []
            for _ in range(3):
                term = rest.astype(jnp.bfloat16).astype(jnp.float32)
                terms.append(term)
                rest = rest - term
            terms.append(jnp.zeros_like(rest))
            o_ref[pl.ds(GROUP, 16), :] = jnp.concatenate(terms, axis=0).astype(jnp.bfloat16)


def attention_cost(heads):
    return pl.CostEstimate(
        flops=heads * 4 * SEQ_HALF * SEQ_HALF * HD, bytes_accessed=2 * 1024 * 1024,
        transcendentals=heads * SEQ_HALF * SEQ_HALF)


def attend_own(where, chunk, q, kv):
    heads = GROUP // HD
    q_spec = pl.BlockSpec((ROWS, HD), lambda h, w: (0, heads * chunk + h))
    k_spec = pl.BlockSpec((ROWS, HD), lambda h, w: (0, h))
    v_spec = pl.BlockSpec((ROWS, HD), lambda h, w: (0, heads + h))
    return pl.pallas_call(
        own_kernel,
        grid_spec=pltpu.PrefetchScalarGridSpec(
            num_scalar_prefetch=1,
            grid=(heads,),
            in_specs=[q_spec] * 4 + [k_spec] * 4 + [v_spec] * 4,
            out_specs=[
                pl.BlockSpec((HD, SEQ_HALF), lambda h, w: (h, 0)),
                pl.BlockSpec((8, SEQ_HALF), lambda h, w: (0, 0)),
            ],
        ),
        out_shape=[
            jax.ShapeDtypeStruct((GROUP, SEQ_HALF), jnp.bfloat16),
            jax.ShapeDtypeStruct((8, SEQ_HALF), jnp.float32),
        ],
        compiler_params=pltpu.CompilerParams(vmem_limit_bytes=24 * 1024 * 1024),
        cost_estimate=attention_cost(heads),
        name="attend_own",
    )(where, *q, *kv, *kv)


def attend_far(where, q, kv):
    heads = GROUP // HD
    q_spec = pl.BlockSpec((SEQ_HALF, HD), lambda h, w: (0, h))
    k_spec = pl.BlockSpec((ROWS, HD), lambda h, w: (0, h))
    v_spec = pl.BlockSpec((ROWS, HD), lambda h, w: (0, heads + h))
    return pl.pallas_call(
        far_kernel,
        grid_spec=pltpu.PrefetchScalarGridSpec(
            num_scalar_prefetch=1,
            grid=(heads,),
            in_specs=[q_spec] + [k_spec] * 4 + [v_spec] * 4,
            out_specs=pl.BlockSpec((GROUP + 16, SEQ_HALF), lambda h, w: (0, 0)),
            scratch_shapes=[pltpu.VMEM((8, SEQ_HALF), jnp.float32)],
        ),
        out_shape=jax.ShapeDtypeStruct((GROUP + 16, SEQ_HALF), jnp.bfloat16),
        compiler_params=pltpu.CompilerParams(vmem_limit_bytes=24 * 1024 * 1024),
        cost_estimate=attention_cost(heads),
        name="attend_far",
    )(where, q, *kv, *kv)


def merge_kernel(where_ref, own_ref, far_ref, own_lse_ref, out_ref):
    terms = far_ref[pl.ds(GROUP, 16), :].astype(jnp.float32)
    far_lse = terms[0:4] + terms[4:8] + terms[8:12]
    far_lse = jnp.where(where_ref[1] == 1, far_lse, -1e30)
    own_lse = own_lse_ref[0:4, :]
    highest = jnp.maximum(own_lse, far_lse)
    own_part = jnp.exp2(own_lse - highest)
    far_part = jnp.exp2(far_lse - highest)
    total = own_part + far_part
    own_part = own_part / total
    far_part = far_part / total
    for head in range(GROUP // HD):
        rows = pl.ds(head * HD, HD)
        mixed = own_ref[rows, :].astype(jnp.float32) * own_part[head : head + 1]
        mixed = mixed + far_ref[rows, :].astype(jnp.float32) * far_part[head : head + 1]
        out_ref[:, rows] = mixed.T.astype(jnp.bfloat16)


def merge(where, own, far, own_lse):
    whole = pl.BlockSpec(memory_space=pltpu.VMEM)
    return pl.pallas_call(
        merge_kernel,
        in_specs=[pl.BlockSpec(memory_space=pltpu.SMEM), whole, whole, whole],
        out_specs=whole,
        out_shape=jax.ShapeDtypeStruct((SEQ_HALF, GROUP), jnp.bfloat16),
        compiler_params=pltpu.CompilerParams(vmem_limit_bytes=16 * 1024 * 1024),
        cost_estimate=pl.CostEstimate(flops=4 * 512 * 512, bytes_accessed=3 * 512 * 1024, transcendentals=0),
        name="merge_halves",
    )(where, own, far, own_lse)


def norm_kernel(where_ref, own_0, own_1, peer_0, peer_1, res_ref, gain_ref, bias_ref, out_ref):
    core = where_ref[2]
    quarter = HALF // 2
    blocks = []
    for half, part, ref in ((core, 0, own_0), (core, 1, own_1), (1 - core, 0, peer_0), (1 - core, 1, peer_1)):
        at = pl.ds(pl.multiple_of(half * HALF + part * quarter, quarter), quarter)
        mixed = deepnorm_alpha * res_ref[:, at].astype(jnp.float32) + ref[...].astype(jnp.float32)
        blocks.append((at, mixed))
    mean = sum(jnp.sum(b, -1, keepdims=True) for _, b in blocks) / D
    blocks = [(at, b - mean) for at, b in blocks]
    var = sum(jnp.sum(b * b, -1, keepdims=True) for _, b in blocks) / D
    inv = lax.rsqrt(var + norm_eps)
    for at, b in blocks:
        out_ref[:, at] = (b * inv * gain_ref[:, at] + bias_ref[:, at]).astype(jnp.bfloat16)


def layer_norm(where, own, peer, residual, gain, bias):
    rows = 32
    part = pl.BlockSpec((rows, HALF // 2), lambda i, w: (i, 0))
    full = pl.BlockSpec((rows, D), lambda i, w: (i, 0))
    vector = pl.BlockSpec((1, D), lambda i, w: (0, 0))
    return pl.pallas_call(
        norm_kernel,
        grid_spec=pltpu.PrefetchScalarGridSpec(
            num_scalar_prefetch=1,
            grid=(ROWS // rows,),
            in_specs=[part] * 4 + [full, vector, vector],
            out_specs=full,
        ),
        out_shape=jax.ShapeDtypeStruct((ROWS, D), jnp.bfloat16),
        compiler_params=pltpu.CompilerParams(vmem_limit_bytes=24 * 1024 * 1024),
        cost_estimate=pl.CostEstimate(flops=10 * ROWS * D, bytes_accessed=6 * ROWS * D, transcendentals=0),
        name="layer_norm",
    )(where, *own, *peer, residual, gain.reshape(1, D), bias.reshape(1, D))


def after(value, *others):
    return lax.optimization_barrier((value, *others))[0]


def exchange_y(arrays, y, starts):
    parts = []
    for step in range(4):
        at = ((y + step) & 3) * GROUP
        part = jnp.concatenate(
            [lax.dynamic_slice_in_dim(a, s + at, GROUP, axis=1) for a, s in zip(arrays, starts)], axis=1
        )
        parts.append(part)
    return [parts[0]] + [lax.ppermute(parts[s], "y", ring(4, s)) for s in (1, 2, 3)]


def gather_weight(weight, s):
    late = (s >> 3) & 1 == 1
    low, high = weight.T[:112], weight.T[112:]
    first = lax.ppermute(jnp.where(late, high, low), ("x", "zl", "c"), spread_pairs(0))
    second = lax.ppermute(jnp.where(late, low, high), ("x", "zl", "c"), spread_pairs(1))
    odd = lax.axis_index("x") & 1 == 1
    part_0 = jnp.where(odd, second, first)
    part_1 = jnp.where(odd, first, second)
    return part_0, part_1


def whole_weight(part):
    return lax.all_gather(part, ("zh", "zl", "x"), axis=0, tiled=True).reshape(2, HALF // 2, GROUP)


def send(block, step):
    return lax.ppermute(block.astype(jnp.bfloat16), "y", ring(4, step))


def local(queries, keys, values, residual_in, out_weight, norm_gain, norm_bias):
    y = lax.axis_index("y")
    zh = lax.axis_index("zh")
    core = lax.axis_index("c")
    where = jnp.stack([y, zh, core]).astype(jnp.int32)
    shard = (lax.axis_index("x") * 4 + lax.axis_index("zl")) * 2 + core

    part_0, part_1 = gather_weight(out_weight, shard)
    weights = [whole_weight(part_0)]
    queries = after(queries, part_0)

    q = exchange_y([queries, queries], y, [0, 2048])
    q_0 = jnp.concatenate([b[:, :GROUP] for b in q], axis=0)
    q_1 = jnp.concatenate([b[:, GROUP:] for b in q], axis=0)
    far_q0 = lax.ppermute(q_0, "zh", [(1, 0)])
    keys, values, _ = lax.optimization_barrier((keys, values, q[2]))
    weights.append(whole_weight(after(part_1, q[2])))
    kv_0 = exchange_y([keys, values], y, [0, 0])
    far_q1 = lax.ppermute(after(q_1, far_q0), "zh", [(1, 0)])
    keys, values, _ = lax.optimization_barrier((keys, values, kv_0[2]))
    kv_1 = exchange_y([keys, values], y, [2048, 2048])

    outs = []
    peers = []
    for chunk, far_q, kv in ((0, far_q0, kv_0), (1, far_q1, kv_1)):
        far_out = attend_far(where, far_q, kv)
        far_out = lax.ppermute(far_out, "zh", [(0, 1)])
        own_out, own_lse = attend_own(where, chunk, q, kv)
        out = merge(where, own_out, far_out, own_lse)
        outs.append(out)
        peers.append(lax.ppermute(out, "c", ring(2, 1)))
    own = jnp.concatenate(outs, 1).reshape(4, ROWS, 2, GROUP)
    other = jnp.concatenate(peers, 1).reshape(4, ROWS, 2, GROUP)

    sums = []
    peer_sums = []
    for weight in weights:

        def project(heads, step):
            return lax.dot_general(
                heads[step], weight, (((1, 2), (0, 2)), ((), ())), preferred_element_type=jnp.float32
            )

        up_1 = send(project(own, 2), 1)
        down_1 = send(project(other, 2), -1)
        up_2 = send(project(other, 3), 1)
        down_2 = send(project(own, 1), -1)
        up_3 = send(project(own, 3) + up_1.astype(jnp.float32), 1)
        down_3 = send(project(other, 1) + down_1.astype(jnp.float32), -1)
        total_other = project(other, 0) + up_2.astype(jnp.float32) + down_3.astype(jnp.float32)
        peer_sums.append(lax.ppermute(total_other.astype(jnp.bfloat16), "c", ring(2, 1)))
        total_own = project(own, 0) + down_2.astype(jnp.float32) + up_3.astype(jnp.float32)
        sums.append(total_own.astype(jnp.bfloat16))
    return layer_norm(where, sums, peer_sums, residual_in, norm_gain, norm_bias)


def solution(mesh):
    fine = Mesh(mesh.devices.reshape(4, 4, 2, 2, 4), AXES)
    tokens = P(AXES, None)
    in_specs = (tokens, tokens, tokens, tokens, P(("zh", "y"), ("x", "zl", "c")), P(), P())
    return jax.shard_map(local, mesh=fine, in_specs=in_specs, out_specs=tokens, check_vma=False)
```

time: 448 us -> 298 us (0.67)
  waiting for transfers between devices: 354 us -> 174 us
  starting transfers between devices: 22.9 us -> 54.8 us
  Pallas kernels: 0 us -> 21.4 us
  local copies, waits for them, and re-layouts: 15.5 us -> 1.87 us
  matrix products: 34.8 us -> 29.9 us
    reduce_scatter x1 -> x0, waiting for transfers between devices: 277 us -> none  [local(): lax.psum_scatter(jnp.dot(attn_heads, group_rows, preferred_element_type=j...]
    all_gather x1 -> x2, waiting for transfers between devices: 7.49 us -> 102 us  [whole_weight(): lax.all_gather(part, ('zh', 'zl', 'x'), axis=0, tiled=True)]
    ppermute x0 -> x31, waiting for transfers between devices: none -> 71.2 us  [the longest x9 22.2 us: exchange_y(): lax.ppermute(parts[s], 'y', ring(4, s))]
    all_to_all x3 -> x0, waiting for transfers between devices: 68.1 us -> none  [the longest x1 28 us: local(): lax.all_to_all(queries, 'ctx', split_axis=1, concat_axis=0, tiled=True)]
    ppermute x0 -> x31, starting transfers between devices: none -> 54.8 us  [the longest x12 15.7 us: send(): return lax.ppermute(block.astype(jnp.bfloat16), 'y', ring(4, step))]
    all_to_all x3 -> x0, starting transfers between devices: 22.9 us -> none  [the longest x1 11.6 us: local(): lax.all_to_all(queries, 'ctx', split_axis=1, concat_axis=0, tiled=True)]
    pallas_call x0 -> x7, Pallas kernels: none -> 21.4 us  [the longest x2 7.83 us: attend_own(): pl.pallas_call(own_kernel, grid_spec=pltpu.PrefetchScalarGridSpec(num_sca...]
    sub x2 -> x0, matrix products: 10.8 us -> none  [one_block(): expo = jnp.exp(scores - highest)]
  transfers between devices with their start and end apart: 5 -> 33, of which waited for: 5 -> 17; matrix products, arithmetic and copies ran while one was open for 8% -> 11% of each run, Pallas kernels for 0% -> 6%
where the time goes in v1:
time: 298 us
  waiting for transfers between devices  174 us (58%)
  starting transfers between devices  54.8 us (18%)
  matrix products  29.9 us (10%)
  Pallas kernels  21.4 us (7%)
  between operations  14.1 us (5%)
    all_gather x2, waiting for transfers between devices, whole_weight(): lax.all_gather(part, ('zh', 'zl', 'x'), axis=0, tiled=True)  102 us
    dot_general x16, matrix products, project(): lax.dot_general(heads[step], weight, (((1, 2), (0, 2)), ((), ())), prefer...  29.9 us
    ppermute x9, waiting for transfers between devices, exchange_y(): lax.ppermute(parts[s], 'y', ring(4, s))  22.2 us
    ppermute x2, waiting for transfers between devices, local(): far_out = lax.ppermute(far_out, 'zh', [(0, 1)])  17.6 us
    ppermute x12, starting transfers between devices, send(): return lax.ppermute(block.astype(jnp.bfloat16), 'y', ring(4, step))  15.7 us
    ppermute x2, starting transfers between devices, local(): lax.ppermute(total_other.astype(jnp.bfloat16), 'c', ring(2, 1))  13 us
    ppermute x12, waiting for transfers between devices, send(): return lax.ppermute(block.astype(jnp.bfloat16), 'y', ring(4, step))  12.4 us
    ppermute x9, starting transfers between devices, exchange_y(): lax.ppermute(parts[s], 'y', ring(4, s))  9.32 us
  transfers between devices with their start and end apart: 33, of which 17 were waited for; matrix products, arithmetic and copies ran while one was open for 11% of the time, Pallas kernels for 6%

profile of v1, /device:TPU:1, one launch (start us, length us, event | category | flops | bytes accessed | tf_op | source)
XLA Modules:
  0.0 298.1 jit_solution(11738823664445447323)
XLA Ops:
  7.5 4.0 %collective-permute-start = (bf16[112,512]{1,0:T(8,128)(2,1)S(1)}, bf16[112,512]{1,0:T(8,128)(2,1)S(1)}, u32[]{:S(2)}, u32[]{:S(2)}) collective-permute-start(bf16[112,512]{1,0:T(8,128)(2,1)S(1)} %get-tuple-element.68), channel_id=1, source_target_pairs={{0,64},{8,192},{16,80},{24,208},{32,96},{40,224},{48,112},{56,240}... | collective-permute-start | bytes 344072 | tf_op jit(solution)/shard_map/ppermute | solution.py:228
  14.0 5.1 %collective-permute-done.1 = bf16[112,512]{1,0:T(8,128)(2,1)S(1)} collective-permute-done((bf16[112,512]{1,0:T(8,128)(2,1)S(1)}, bf16[112,512]{1,0:T(8,128)(2,1)S(1)}, u32[]{:S(2)}, u32[]{:S(2)}) %collective-permute-start.1) | collective-permute-done | bytes 114720 | tf_op jit(solution)/shard_map/ppermute | solution.py:227
  21.3 3.0 %collective-permute-start.3 = (bf16[128,1024]{1,0:T(8,128)(2,1)S(1)}, bf16[128,1024]{1,0:T(8,128)(2,1)S(1)}, u32[]{:S(2)}, u32[]{:S(2)}) collective-permute-start(bf16[128,1024]{1,0:T(8,128)(2,1)S(1)} %pad_maximum_fusion.5), channel_id=1, source_target_pairs={{0,2},{1,3},{2,0},{3,1},{4,6},{5,7},{6,4},{7,5},{8,10},{9,11},{10,... | collective-permute-start | bytes 786440 | tf_op jit(solution)/shard_map/ppermute | solution.py:221
  24.3 3.8 %collective-permute-done.3.refs_2_ = bf16[128,1024]{1,0:T(8,128)(2,1)S(1)} collective-permute-done((bf16[128,1024]{1,0:T(8,128)(2,1)S(1)}, bf16[128,1024]{1,0:T(8,128)(2,1)S(1)}, u32[]{:S(2)}, u32[]{:S(2)}) %collective-permute-start.3) | collective-permute-done | bytes 262176 | tf_op jit(solution)/shard_map/ppermute | solution.py:221
  28.2 2.8 collective-permute-start.4
  31.2 3.4 %collective-permute-done.4.refs_3_ = bf16[128,1024]{1,0:T(8,128)(2,1)S(1)} collective-permute-done((bf16[128,1024]{1,0:T(8,128)(2,1)S(1)}, bf16[128,1024]{1,0:T(8,128)(2,1)S(1)}, u32[]{:S(2)}, u32[]{:S(2)}) %collective-permute-start.4) | collective-permute-done | bytes 262176 | tf_op jit(solution)/shard_map/ppermute | solution.py:221
  34.6 3.4 %collective-permute-done.2.refs_1_ = bf16[128,1024]{1,0:T(8,128)(2,1)S(1)} collective-permute-done((bf16[128,1024]{1,0:T(8,128)(2,1)S(1)}, bf16[128,1024]{1,0:T(8,128)(2,1)S(1)}, u32[]{:S(2)}, u32[]{:S(2)}) %collective-permute-start.2) | collective-permute-done | bytes 262176 | tf_op jit(solution)/shard_map/ppermute | solution.py:221
  41.4 8.1 %collective-permute-done.6.refs_6_.refs_10_.refs_2_ = bf16[128,1024]{1,0:T(8,128)(2,1)S(1)} collective-permute-done((bf16[128,1024]{1,0:T(8,128)(2,1)S(1)}, bf16[128,1024]{1,0:T(8,128)(2,1)S(1)}, u32[]{:S(2)}, u32[]{:S(2)}) %collective-permute-start.6) | collective-permute-done | bytes 262176 | tf_op jit(solution)/shard_map/ppermute | solution.py:221
  49.6 7.9 %collective-permute-done.8.q_ref = bf16[512,512]{1,0:T(8,128)(2,1)S(1)} collective-permute-done((bf16[512,512]{1,0:T(8,128)(2,1)S(1)}, bf16[512,512]{1,0:T(8,128)(2,1)S(1)}, u32[]{:S(2)}, u32[]{:S(2)}) %collective-permute-start.8) | collective-permute-done | bytes 524320 | tf_op jit(solution)/shard_map/ppermute | solution.py:257
  60.6 3.9 %attend_far.2 = bf16[528,512]{1,0:T(8,128)(2,1)S(1)} custom-call(s32[3]{0:T(128)S(1)} %pad_add_fusion.where_ref, bf16[512,512]{1,0:T(8,128)(2,1)S(1)} %collective-permute-done.8.q_ref, bf16[128,1024]{1,0:T(8,128)(2,1)S(1)} %pad_maximum_fusion.7.refs_4_.refs_8_.refs_0_, bf16[128,1024]{1,0:T(8,128)(2,1)S(1)} %collective-permute-done.5.refs_5_.refs_9_.refs_1_, ...), custom_call_target="tpu_custom_call" | custom-call | flops 536870912 | bytes 2097152 | tf_op jit(solution)/shard_map/attend_far/pallas_call | solution.py:126
  64.5 5.1 %collective-permute-start.9 = (bf16[528,512]{1,0:T(8,128)(2,1)S(1)}, bf16[528,512]{1,0:T(8,128)(2,1)S(1)}, u32[]{:S(2)}, u32[]{:S(2)}) collective-permute-start(bf16[528,512]{1,0:T(8,128)(2,1)S(1)} %attend_far.2), channel_id=1, source_target_pairs={{0,4},{1,5},{2,6},{3,7},{8,12},{9,13},{10,14},{11,15},{16,20},{17,... | collective-permute-start | bytes 1622024 | tf_op jit(solution)/shard_map/ppermute | solution.py:269
  69.7 3.4 %collective-permute-done.10.refs_5_.refs_9_.refs_1_ = bf16[128,1024]{1,0:T(8,128)(2,1)S(1)} collective-permute-done((bf16[128,1024]{1,0:T(8,128)(2,1)S(1)}, bf16[128,1024]{1,0:T(8,128)(2,1)S(1)}, u32[]{:S(2)}, u32[]{:S(2)}) %collective-permute-start.10) | collective-permute-done | bytes 262176 | tf_op jit(solution)/shard_map/ppermute | solution.py:221
  73.2 2.9 collective-permute-done.13.q_ref
  76.1 3.9 %attend_far.3 = bf16[528,512]{1,0:T(8,128)(2,1)S(1)} custom-call(s32[3]{0:T(128)S(1)} %pad_add_fusion.where_ref, bf16[512,512]{1,0:T(8,128)(2,1)S(1)} %collective-permute-done.13.q_ref, bf16[128,1024]{1,0:T(8,128)(2,1)S(1)} %pad_maximum_fusion.11.refs_4_.refs_8_.refs_0_, bf16[128,1024]{1,0:T(8,128)(2,1)S(1)} %collective-permute-done.10.refs_5_.refs_9_.refs_1_, ...), custom_call_target="tpu_custom_call" | custom-call | flops 536870912 | bytes 2097152 | tf_op jit(solution)/shard_map/attend_far/pallas_call | solution.py:126
  80.0 2.4 collective-permute-start.14
  82.4 3.9 %attend_own.2 = (bf16[512,512]{1,0:T(8,128)(2,1)S(1)}, f32[8,512]{1,0:T(8,128)S(1)}) custom-call(s32[3]{0:T(128)S(1)} %pad_add_fusion.where_ref, bf16[128,1024]{1,0:T(8,128)(2,1)S(1)} %pad_maximum_fusion.3.refs_0_, bf16[128,1024]{1,0:T(8,128)(2,1)S(1)} %collective-permute-done.2.refs_1_, bf16[128,1024]{1,0:T(8,128)(2,1)S(1)} %collective-permute-done.3.refs_2_, ...), custom_call_target="tpu_custom_call" | custom-call | flops 536870912 | bytes 2097152 | tf_op jit(solution)/shard_map/attend_own/pallas_call | solution.py:100
  88.2 3.9 %attend_own.3 = (bf16[512,512]{1,0:T(8,128)(2,1)S(1)}, f32[8,512]{1,0:T(8,128)S(1)}) custom-call(s32[3]{0:T(128)S(1)} %pad_add_fusion.where_ref, bf16[128,1024]{1,0:T(8,128)(2,1)S(1)} %pad_maximum_fusion.3.refs_0_, bf16[128,1024]{1,0:T(8,128)(2,1)S(1)} %collective-permute-done.2.refs_1_, bf16[128,1024]{1,0:T(8,128)(2,1)S(1)} %collective-permute-done.3.refs_2_, ...), custom_call_target="tpu_custom_call" | custom-call | flops 536870912 | bytes 2097152 | tf_op jit(solution)/shard_map/attend_own/pallas_call | solution.py:100
  92.1 16.9 %collective-permute-done.14.far_ref = bf16[528,512]{1,0:T(8,128)(2,1)S(1)} collective-permute-done((bf16[528,512]{1,0:T(8,128)(2,1)S(1)}, bf16[528,512]{1,0:T(8,128)(2,1)S(1)}, u32[]{:S(2)}, u32[]{:S(2)}) %collective-permute-start.14) | collective-permute-done | bytes 540704 | tf_op jit(solution)/shard_map/ppermute | solution.py:269
  112.1 36.3 %all-gather.3.cloned.1.call-done = bf16[3584,512]{1,0:T(8,128)(2,1)} async-done(((bf16[112,512]{1,0:T(8,128)(2,1)}), bf16[3584,512]{1,0:T(8,128)(2,1)}) %all-gather.3.cloned.1.call-update) | async-done | bytes 3670032 | tf_op jit(solution)/shard_map/all_gather | solution.py:236
  148.3 4.3 %fusion.13 = bf16[128,1792]{1,0:T(8,128)(2,1)} fusion(bf16[2,1792,512]{2,1,0:T(8,128)(2,1)} %bitcast.150, bf16[16,2,8,512]{3,2,1,0:T(8,128)(2,1)S(1)} %bitcast.176), kind=kOutput, calls=%fused_computation.29 | convolution fusion | flops 469991424 | bytes 4390912 | tf_op jit(solution)/shard_map/dot_general | solution.py:282
  152.6 2.9 collective-permute-start.24
  163.1 66.1 %all-gather.5.cloned.1.call-done = bf16[3584,512]{1,0:T(8,128)(2,1)} async-done(((bf16[112,512]{1,0:T(8,128)(2,1)}), bf16[3584,512]{1,0:T(8,128)(2,1)}) %all-gather.5.cloned.1.call-update) | async-done | bytes 3670032 | tf_op jit(solution)/shard_map/all_gather | solution.py:236
  229.2 3.5 %fusion.15 = bf16[128,1792]{1,0:T(8,128)(2,1)S(1)} fusion(bf16[2,1792,512]{2,1,0:T(8,128)(2,1)} %bitcast.158, bf16[16,2,8,512]{3,2,1,0:T(8,128)(2,1)S(1)} %bitcast.177), kind=kOutput, calls=%fused_computation.31 | convolution fusion | flops 469991424 | bytes 4390912 | tf_op jit(solution)/shard_map/dot_general | solution.py:282
  236.6 2.5 collective-permute-start.28
  242.1 2.3 fusion.6
  246.0 2.6 collective-permute-start.25
  249.9 11.0 %collective-permute-done.19 = bf16[128,1792]{1,0:T(8,128)(2,1)S(1)} collective-permute-done((bf16[128,1792]{1,0:T(8,128)(2,1)S(1)}, bf16[128,1792]{1,0:T(8,128)(2,1)S(1)}, u32[]{:S(2)}, u32[]{:S(2)}) %collective-permute-start.19) | collective-permute-done | bytes 458784 | tf_op jit(solution)/shard_map/ppermute | solution.py:240
  262.3 2.7 collective-permute-start.18
  265.1 2.4 fusion.16
  270.3 10.8 %collective-permute-start.26 = (bf16[128,1792]{1,0:T(8,128)(2,1)S(1)}, bf16[128,1792]{1,0:T(8,128)(2,1)S(1)}, u32[]{:S(2)}, u32[]{:S(2)}) collective-permute-start(bf16[128,1792]{1,0:T(8,128)(2,1)S(1)} %fusion.16), channel_id=1, source_target_pairs={{0,8},{8,0},{1,9},{9,1},{2,10},{10,2},{3,11},{11,3},{4,12},{12,4},... | collective-permute-start | bytes 1376264 | tf_op jit(solution)/shard_map/ppermute | solution.py:293
  281.1 2.3 fusion.17.own_0
  287.2 4.0 %layer_norm.1 = bf16[128,7168]{1,0:T(8,128)(2,1)} custom-call(s32[3]{0:T(128)S(1)} %pad_add_fusion.where_ref, bf16[128,1792]{1,0:T(8,128)(2,1)S(1)} %fusion.17.own_0, bf16[128,1792]{1,0:T(8,128)(2,1)S(1)} %add_convert_fusion.2.own_1, bf16[128,1792]{1,0:T(8,128)(2,1)S(1)} %collective-permute-done.26.peer_0, ...), custom_call_target="tpu_custom_call" | custom-call | flops 9175040 | bytes 5505024 | tf_op jit(solution)/shard_map/layer_norm/pallas_call | solution.py:194
  (105 shorter events, 42.3 us)
Async XLA Ops:
  6.5 141.8 %all-gather.3.cloned.1.call-start = ((), (), s32[]{:S(2)}) async-start(), calls=%async_computation | async-start | bytes 3784704 | tf_op jit(solution)/shard_map/all_gather | solution.py:236
  7.5 6.4 %collective-permute-start = (bf16[112,512]{1,0:T(8,128)(2,1)S(1)}, bf16[112,512]{1,0:T(8,128)(2,1)S(1)}, u32[]{:S(2)}, u32[]{:S(2)}) collective-permute-start(bf16[112,512]{1,0:T(8,128)(2,1)S(1)} %get-tuple-element.68), channel_id=1, source_target_pairs={{0,64},{8,192},{16,80},{24,208},{32,96},{40,224},{48,112},{56,240}... | collective-permute-start | bytes 344072 | tf_op jit(solution)/shard_map/ppermute | solution.py:228
  11.5 7.6 %collective-permute-start.1 = (bf16[112,512]{1,0:T(8,128)(2,1)S(1)}, bf16[112,512]{1,0:T(8,128)(2,1)S(1)}, u32[]{:S(2)}, u32[]{:S(2)}) collective-permute-start(bf16[112,512]{1,0:T(8,128)(2,1)S(1)} %get-tuple-element.67), channel_id=1, source_target_pairs={{0,0},{8,128},{16,16},{24,144},{32,32},{40,160},{48,48},{56,176},{... | collective-permute-start | bytes 344072 | tf_op jit(solution)/shard_map/ppermute | solution.py:227
  19.8 209.4 %all-gather.5.cloned.1.call-start = ((), (), s32[]{:S(2)}) async-start(), calls=%async_computation.1 | async-start | bytes 3784704 | tf_op jit(solution)/shard_map/all_gather | solution.py:236
  21.3 6.8 %collective-permute-start.3 = (bf16[128,1024]{1,0:T(8,128)(2,1)S(1)}, bf16[128,1024]{1,0:T(8,128)(2,1)S(1)}, u32[]{:S(2)}, u32[]{:S(2)}) collective-permute-start(bf16[128,1024]{1,0:T(8,128)(2,1)S(1)} %pad_maximum_fusion.5), channel_id=1, source_target_pairs={{0,2},{1,3},{2,0},{3,1},{4,6},{5,7},{6,4},{7,5},{8,10},{9,11},{10,... | collective-permute-start | bytes 786440 | tf_op jit(solution)/shard_map/ppermute | solution.py:221
  28.2 6.4 %collective-permute-start.4 = (bf16[128,1024]{1,0:T(8,128)(2,1)S(1)}, bf16[128,1024]{1,0:T(8,128)(2,1)S(1)}, u32[]{:S(2)}, u32[]{:S(2)}) collective-permute-start(bf16[128,1024]{1,0:T(8,128)(2,1)S(1)} %pad_maximum_fusion.6), channel_id=1, source_target_pairs={{0,3},{1,0},{2,1},{3,2},{4,7},{5,4},{6,5},{7,6},{8,11},{9,8},{10,9... | collective-permute-start | bytes 786440 | tf_op jit(solution)/shard_map/ppermute | solution.py:221
  31.1 6.9 %collective-permute-start.2 = (bf16[128,1024]{1,0:T(8,128)(2,1)S(1)}, bf16[128,1024]{1,0:T(8,128)(2,1)S(1)}, u32[]{:S(2)}, u32[]{:S(2)}) collective-permute-start(bf16[128,1024]{1,0:T(8,128)(2,1)S(1)} %pad_maximum_fusion.4), channel_id=1, source_target_pairs={{0,1},{1,2},{2,3},{3,0},{4,5},{5,6},{6,7},{7,4},{8,9},{9,10},{10,1... | collective-permute-start | bytes 786440 | tf_op jit(solution)/shard_map/ppermute | solution.py:221
  38.1 19.4 %collective-permute-start.8 = (bf16[512,512]{1,0:T(8,128)(2,1)S(1)}, bf16[512,512]{1,0:T(8,128)(2,1)S(1)}, u32[]{:S(2)}, u32[]{:S(2)}) collective-permute-start(bf16[512,512]{1,0:T(8,128)(2,1)S(1)} %pad_maximum_fusion), channel_id=1, source_target_pairs={{4,0},{5,1},{6,2},{7,3},{12,8},{13,9},{14,10},{15,11},{20,16},{21,... | collective-permute-start | bytes 1572872 | tf_op jit(solution)/shard_map/ppermute | solution.py:257
  39.5 10.0 %collective-permute-start.6 = (bf16[128,1024]{1,0:T(8,128)(2,1)S(1)}, bf16[128,1024]{1,0:T(8,128)(2,1)S(1)}, u32[]{:S(2)}, u32[]{:S(2)}) collective-permute-start(bf16[128,1024]{1,0:T(8,128)(2,1)S(1)} %pad_maximum_fusion.9), channel_id=1, source_target_pairs={{0,2},{1,3},{2,0},{3,1},{4,6},{5,7},{6,4},{7,5},{8,10},{9,11},{10,... | collective-permute-start | bytes 786440 | tf_op jit(solution)/shard_map/ppermute | solution.py:221
  39.7 19.6 %collective-permute-start.7 = (bf16[128,1024]{1,0:T(8,128)(2,1)S(1)}, bf16[128,1024]{1,0:T(8,128)(2,1)S(1)}, u32[]{:S(2)}, u32[]{:S(2)}) collective-permute-start(bf16[128,1024]{1,0:T(8,128)(2,1)S(1)} %pad_maximum_fusion.10), channel_id=1, source_target_pairs={{0,3},{1,0},{2,1},{3,2},{4,7},{5,4},{6,5},{7,6},{8,11},{9,8},{10,9... | collective-permute-start | bytes 786440 | tf_op jit(solution)/shard_map/ppermute | solution.py:221
  40.5 20.1 %collective-permute-start.5 = (bf16[128,1024]{1,0:T(8,128)(2,1)S(1)}, bf16[128,1024]{1,0:T(8,128)(2,1)S(1)}, u32[]{:S(2)}, u32[]{:S(2)}) collective-permute-start(bf16[128,1024]{1,0:T(8,128)(2,1)S(1)} %pad_maximum_fusion.8), channel_id=1, source_target_pairs={{0,1},{1,2},{2,3},{3,0},{4,5},{5,6},{6,7},{7,4},{8,9},{9,10},{10,1... | collective-permute-start | bytes 786440 | tf_op jit(solution)/shard_map/ppermute | solution.py:221
  57.5 18.6 %collective-permute-start.13 = (bf16[512,512]{1,0:T(8,128)(2,1)S(1)}, bf16[512,512]{1,0:T(8,128)(2,1)S(1)}, u32[]{:S(2)}, u32[]{:S(2)}) collective-permute-start(bf16[512,512]{1,0:T(8,128)(2,1)S(1)} %pad_maximum_fusion.1), channel_id=1, source_target_pairs={{4,0},{5,1},{6,2},{7,3},{12,8},{13,9},{14,10},{15,11},{20,16},{21,... | collective-permute-start | bytes 1572872 | tf_op jit(solution)/shard_map/ppermute | solution.py:261
  58.8 10.9 %collective-permute-start.12 = (bf16[128,1024]{1,0:T(8,128)(2,1)S(1)}, bf16[128,1024]{1,0:T(8,128)(2,1)S(1)}, u32[]{:S(2)}, u32[]{:S(2)}) collective-permute-start(bf16[128,1024]{1,0:T(8,128)(2,1)S(1)} %pad_maximum_fusion.14), channel_id=1, source_target_pairs={{0,3},{1,0},{2,1},{3,2},{4,7},{5,4},{6,5},{7,6},{8,11},{9,8},{10,9... | collective-permute-start | bytes 786440 | tf_op jit(solution)/shard_map/ppermute | solution.py:221
  58.9 10.8 %collective-permute-start.11 = (bf16[128,1024]{1,0:T(8,128)(2,1)S(1)}, bf16[128,1024]{1,0:T(8,128)(2,1)S(1)}, u32[]{:S(2)}, u32[]{:S(2)}) collective-permute-start(bf16[128,1024]{1,0:T(8,128)(2,1)S(1)} %pad_maximum_fusion.13), channel_id=1, source_target_pairs={{0,2},{1,3},{2,0},{3,1},{4,6},{5,7},{6,4},{7,5},{8,10},{9,11},{10,... | collective-permute-start | bytes 786440 | tf_op jit(solution)/shard_map/ppermute | solution.py:221
  59.3 13.9 %collective-permute-start.10 = (bf16[128,1024]{1,0:T(8,128)(2,1)S(1)}, bf16[128,1024]{1,0:T(8,128)(2,1)S(1)}, u32[]{:S(2)}, u32[]{:S(2)}) collective-permute-start(bf16[128,1024]{1,0:T(8,128)(2,1)S(1)} %pad_maximum_fusion.12), channel_id=1, source_target_pairs={{0,1},{1,2},{2,3},{3,0},{4,5},{5,6},{6,7},{7,4},{8,9},{9,10},{10,1... | collective-permute-start | bytes 786440 | tf_op jit(solution)/shard_map/ppermute | solution.py:221
  64.5 22.5 %collective-permute-start.9 = (bf16[528,512]{1,0:T(8,128)(2,1)S(1)}, bf16[528,512]{1,0:T(8,128)(2,1)S(1)}, u32[]{:S(2)}, u32[]{:S(2)}) collective-permute-start(bf16[528,512]{1,0:T(8,128)(2,1)S(1)} %attend_far.2), channel_id=1, source_target_pairs={{0,4},{1,5},{2,6},{3,7},{8,12},{9,13},{10,14},{11,15},{16,20},{17,... | collective-permute-start | bytes 1622024 | tf_op jit(solution)/shard_map/ppermute | solution.py:269
  80.0 29.0 %collective-permute-start.14 = (bf16[528,512]{1,0:T(8,128)(2,1)S(1)}, bf16[528,512]{1,0:T(8,128)(2,1)S(1)}, u32[]{:S(2)}, u32[]{:S(2)}) collective-permute-start(bf16[528,512]{1,0:T(8,128)(2,1)S(1)} %attend_far.3), channel_id=1, source_target_pairs={{0,4},{1,5},{2,6},{3,7},{8,12},{9,13},{10,14},{11,15},{16,20},{17,... | collective-permute-start | bytes 1622024 | tf_op jit(solution)/shard_map/ppermute | solution.py:269
  87.9 22.1 %collective-permute-start.21 = (bf16[512,512]{1,0:T(8,128)(2,1)S(1)}, bf16[512,512]{1,0:T(8,128)(2,1)S(1)}, u32[]{:S(2)}, u32[]{:S(2)}) collective-permute-start(bf16[512,512]{1,0:T(8,128)(2,1)S(1)} %merge_halves.2), channel_id=1, source_target_pairs={{0,8},{8,0},{1,9},{9,1},{2,10},{10,2},{3,11},{11,3},{4,12},{12,4},... | collective-permute-start | bytes 1572872 | tf_op jit(solution)/shard_map/ppermute | solution.py:273
  152.6 89.2 %collective-permute-start.24 = (bf16[128,1792]{1,0:T(8,128)(2,1)}, bf16[128,1792]{1,0:T(8,128)(2,1)}, u32[]{:S(2)}, u32[]{:S(2)}) collective-permute-start(bf16[128,1792]{1,0:T(8,128)(2,1)} %fusion.13), channel_id=1, source_target_pairs={{0,3},{1,0},{2,1},{3,2},{4,7},{5,4},{6,5},{7,6},{8,11},{9,8},{10,9... | collective-permute-start | bytes 1376264 | tf_op jit(solution)/shard_map/ppermute | solution.py:240
  156.8 105.4 %collective-permute-start.23 = (bf16[128,1792]{1,0:T(8,128)(2,1)S(1)}, bf16[128,1792]{1,0:T(8,128)(2,1)}, u32[]{:S(2)}, u32[]{:S(2)}) collective-permute-start(bf16[128,1792]{1,0:T(8,128)(2,1)S(1)} %fusion.12), channel_id=1, source_target_pairs={{0,1},{1,2},{2,3},{3,0},{4,5},{5,6},{6,7},{7,4},{8,9},{9,10},{10,1... | collective-permute-start | bytes 1376264 | tf_op jit(solution)/shard_map/ppermute | solution.py:240
  159.0 85.4 %collective-permute-start.16 = (bf16[128,1792]{1,0:T(8,128)(2,1)}, bf16[128,1792]{1,0:T(8,128)(2,1)S(1)}, u32[]{:S(2)}, u32[]{:S(2)}) collective-permute-start(bf16[128,1792]{1,0:T(8,128)(2,1)} %fusion.9), channel_id=1, source_target_pairs={{0,1},{1,2},{2,3},{3,0},{4,5},{5,6},{6,7},{7,4},{8,9},{9,10},{10,1... | collective-permute-start | bytes 1376264 | tf_op jit(solution)/shard_map/ppermute | solution.py:240
  161.8 105.7 %collective-permute-start.15 = (bf16[128,1792]{1,0:T(8,128)(2,1)S(1)}, bf16[128,1792]{1,0:T(8,128)(2,1)}, u32[]{:S(2)}, u32[]{:S(2)}) collective-permute-start(bf16[128,1792]{1,0:T(8,128)(2,1)S(1)} %fusion.8), channel_id=1, source_target_pairs={{0,3},{1,0},{2,1},{3,2},{4,7},{5,4},{6,5},{7,6},{8,11},{9,8},{10,9... | collective-permute-start | bytes 1376264 | tf_op jit(solution)/shard_map/ppermute | solution.py:240
  236.6 9.4 %collective-permute-start.28 = (bf16[128,1792]{1,0:T(8,128)(2,1)S(1)}, bf16[128,1792]{1,0:T(8,128)(2,1)S(1)}, u32[]{:S(2)}, u32[]{:S(2)}) collective-permute-start(bf16[128,1792]{1,0:T(8,128)(2,1)S(1)} %fusion.15), channel_id=1, source_target_pairs={{0,3},{1,0},{2,1},{3,2},{4,7},{5,4},{6,5},{7,6},{8,11},{9,8},{10,9... | collective-permute-start | bytes 1376264 | tf_op jit(solution)/shard_map/ppermute | solution.py:240
  241.8 41.6 %collective-permute-start.27 = (bf16[128,1792]{1,0:T(8,128)(2,1)S(1)}, bf16[128,1792]{1,0:T(8,128)(2,1)S(1)}, u32[]{:S(2)}, u32[]{:S(2)}) collective-permute-start(bf16[128,1792]{1,0:T(8,128)(2,1)S(1)} %fusion.14), channel_id=1, source_target_pairs={{0,1},{1,2},{2,3},{3,0},{4,5},{5,6},{6,7},{7,4},{8,9},{9,10},{10,1... | collective-permute-start | bytes 1376264 | tf_op jit(solution)/shard_map/ppermute | solution.py:240
  244.4 16.5 %collective-permute-start.19 = (bf16[128,1792]{1,0:T(8,128)(2,1)S(1)}, bf16[128,1792]{1,0:T(8,128)(2,1)S(1)}, u32[]{:S(2)}, u32[]{:S(2)}) collective-permute-start(bf16[128,1792]{1,0:T(8,128)(2,1)S(1)} %fusion.11), channel_id=1, source_target_pairs={{0,1},{1,2},{2,3},{3,0},{4,5},{5,6},{6,7},{7,4},{8,9},{9,10},{10,1... | collective-permute-start | bytes 1376264 | tf_op jit(solution)/shard_map/ppermute | solution.py:240
  246.0 19.0 %collective-permute-start.25 = (bf16[128,1792]{1,0:T(8,128)(2,1)S(1)}, bf16[128,1792]{1,0:T(8,128)(2,1)S(1)}, u32[]{:S(2)}, u32[]{:S(2)}) collective-permute-start(bf16[128,1792]{1,0:T(8,128)(2,1)S(1)} %fusion.6), channel_id=1, source_target_pairs={{0,3},{1,0},{2,1},{3,2},{4,7},{5,4},{6,5},{7,6},{8,11},{9,8},{10,9... | collective-permute-start | bytes 1376264 | tf_op jit(solution)/shard_map/ppermute | solution.py:240
  260.9 9.3 %collective-permute-start.17 = (bf16[128,1792]{1,0:T(8,128)(2,1)S(1)}, bf16[128,1792]{1,0:T(8,128)(2,1)S(1)}, u32[]{:S(2)}, u32[]{:S(2)}) collective-permute-start(bf16[128,1792]{1,0:T(8,128)(2,1)S(1)} %fusion.7), channel_id=1, source_target_pairs={{0,1},{1,2},{2,3},{3,0},{4,5},{5,6},{6,7},{7,4},{8,9},{9,10},{10,1... | collective-permute-start | bytes 1376264 | tf_op jit(solution)/shard_map/ppermute | solution.py:240
  262.3 23.5 %collective-permute-start.18 = (bf16[128,1792]{1,0:T(8,128)(2,1)S(1)}, bf16[128,1792]{1,0:T(8,128)(2,1)S(1)}, u32[]{:S(2)}, u32[]{:S(2)}) collective-permute-start(bf16[128,1792]{1,0:T(8,128)(2,1)S(1)} %fusion.10), channel_id=1, source_target_pairs={{0,3},{1,0},{2,1},{3,2},{4,7},{5,4},{6,5},{7,6},{8,11},{9,8},{10,9... | collective-permute-start | bytes 1376264 | tf_op jit(solution)/shard_map/ppermute | solution.py:240
  265.0 18.4 %collective-permute-start.29 = (bf16[128,1792]{1,0:T(8,128)(2,1)S(1)}, bf16[128,1792]{1,0:T(8,128)(2,1)S(1)}, u32[]{:S(2)}, u32[]{:S(2)}) collective-permute-start(bf16[128,1792]{1,0:T(8,128)(2,1)S(1)} %add_convert_fusion.1), channel_id=1, source_target_pairs={{0,3},{1,0},{2,1},{3,2},{4,7},{5,4},{6,5},{7,6},{8,11},{9,8},{10,9... | collective-permute-start | bytes 1376264 | tf_op jit(solution)/shard_map/ppermute | solution.py:240
  267.5 18.3 %collective-permute-start.20 = (bf16[128,1792]{1,0:T(8,128)(2,1)S(1)}, bf16[128,1792]{1,0:T(8,128)(2,1)S(1)}, u32[]{:S(2)}, u32[]{:S(2)}) collective-permute-start(bf16[128,1792]{1,0:T(8,128)(2,1)S(1)} %add_convert_fusion.3), channel_id=1, source_target_pairs={{0,1},{1,2},{2,3},{3,0},{4,5},{5,6},{6,7},{7,4},{8,9},{9,10},{10,1... | collective-permute-start | bytes 1376264 | tf_op jit(solution)/shard_map/ppermute | solution.py:240
  270.3 15.7 %collective-permute-start.26 = (bf16[128,1792]{1,0:T(8,128)(2,1)S(1)}, bf16[128,1792]{1,0:T(8,128)(2,1)S(1)}, u32[]{:S(2)}, u32[]{:S(2)}) collective-permute-start(bf16[128,1792]{1,0:T(8,128)(2,1)S(1)} %fusion.16), channel_id=1, source_target_pairs={{0,8},{8,0},{1,9},{9,1},{2,10},{10,2},{3,11},{11,3},{4,12},{12,4},... | collective-permute-start | bytes 1376264 | tf_op jit(solution)/shard_map/ppermute | solution.py:293
  283.6 3.7 %collective-permute-start.30 = (bf16[128,1792]{1,0:T(8,128)(2,1)S(1)}, bf16[128,1792]{1,0:T(8,128)(2,1)S(1)}, u32[]{:S(2)}, u32[]{:S(2)}) collective-permute-start(bf16[128,1792]{1,0:T(8,128)(2,1)S(1)} %add_convert_fusion), channel_id=1, source_target_pairs={{0,8},{8,0},{1,9},{9,1},{2,10},{10,2},{3,11},{11,3},{4,12},{12,4},... | collective-permute-start | bytes 1376264 | tf_op jit(solution)/shard_map/ppermute | solution.py:293
  (9 other events, 138.6 us)
Sparse Core Ops, SparseCore 0:
  19.9 128.3 all-gather.2
  150.9 78.2 all-gather.4
